TPU v7x, 256 devices: a whole 4x4x8 slice. The times are simulated.
256 devices in a mesh: blk: 64 (over x, z, core), sub: 4 (over y).
Axes of the slice: x: 4, y: 4, z: 8, core: 2. Of those that a mesh axis runs over, the one named last changes fastest.
Arguments:
- features: bfloat16 [16, 524288], P(None, 'blk'), may hold values from -6 to 6
- probes: bfloat16 [8, 524288], P(None, 'blk'), may hold values from -0.59765625 to 0.59765625
- inv_scale: float32 [16], replicated, may hold values from 0.025 to 0.1
- tile_rows: int32 [8192], replicated, may hold values from 0 to 511, as said below
- tile_cols: int32 [8192], replicated, may hold values from 0 to 511, as said below
Outputs:
- responses: float32 [8, 524288], P(None, ('blk', 'sub'))
Inputs may be any that keep to these rules, and one draw needn't show every extreme that they name: `tile_rows`: block ids. Tiles h * 32 to (h + 1) * 32 - 1 belong to helper h, the device with flat index h over blk+sub. Block b lies on owner b // 8. Of the 32 row and 32 column blocks of one helper together, at most 1 lie on one owner, and some owner holds exactly 1; of its row blocks alone, at most 1 lie on one owner, and some owner holds exactly 1. `tile_cols`: block ids, as for tile_rows; of one helper's column blocks, at most 1 lie on one owner, and some owner holds exactly 1.
All inputs are finite; a program needn't handle non-finite values.
Results may differ from a plain program's by a relative error of at most 0.0051.
Values may be sent and summed in bfloat16 or wider, within the bound.
A program may use at most 128 MiB of HBM per device.

v0:
```python
import jax
import jax.numpy as jnp
from jax import lax
from jax.sharding import PartitionSpec as P

BS = 1024
TILES_DEV = 32


def wendland(distance):
    remain = jnp.maximum(1.0 - distance, 0.0)
    square = remain * remain
    fourth = square * square
    eighth = fourth * fourth
    return eighth * square * remain * (11.0 * distance + 1.0)


def scale_rows(data, inv_scale, feature_count):
    scaled = (data[:feature_count].astype(jnp.float32) * inv_scale[:, None]).astype(jnp.bfloat16)
    scaled = lax.optimization_barrier(scaled)
    widened = scaled.astype(jnp.float32)
    return (scaled, jnp.sum(widened * widened, axis=0))


def tile_response(row_data, col_data, inv_scale, feature_count):
    row_scaled, row_sq = scale_rows(row_data, inv_scale, feature_count)
    col_scaled, col_sq = scale_rows(col_data, inv_scale, feature_count)
    gram_tile = lax.dot_general(
        col_scaled, row_scaled, (((0,), (0,)), ((), ())), preferred_element_type=jnp.float32
    )
    distance = jnp.sqrt(jnp.maximum(col_sq[:, None] + row_sq[None, :] - 2.0 * gram_tile, 0.0))
    kernel = wendland(distance).astype(jnp.bfloat16)
    return jnp.dot(col_data[feature_count:], kernel, preferred_element_type=jnp.float32)


def rank_among(owners):
    entries = owners.shape[-1]
    same_owner = owners[..., :, None] == owners[..., None, :]
    earlier = lax.broadcasted_iota(jnp.int32, (entries, entries), 1) < lax.broadcasted_iota(
        jnp.int32, (entries, entries), 0
    )
    return jnp.sum(jnp.logical_and(same_owner, earlier), axis=-1)


def per_device(features, probes, inv_scale, tile_rows, tile_cols):
    n_blk = lax.axis_size("blk")
    n_sub = lax.axis_size("sub")
    blk_index = lax.axis_index("blk")
    sub_index = lax.axis_index("sub")
    feature_count = features.shape[0]
    owned_blocks = features.shape[1] // BS
    stacked = jnp.concatenate([features, probes], axis=0)
    stack_rows = stacked.shape[0]
    own_data = jnp.transpose(stacked.reshape(stack_rows, owned_blocks, BS), (1, 0, 2))
    column_rows = lax.dynamic_index_in_dim(
        tile_rows.reshape(n_blk, n_sub, TILES_DEV), sub_index, 1, keepdims=False
    )
    column_cols = lax.dynamic_index_in_dim(
        tile_cols.reshape(n_blk, n_sub, TILES_DEV), sub_index, 1, keepdims=False
    )
    column_ends = jnp.concatenate([column_rows, column_cols], axis=1)
    my_ends = lax.dynamic_index_in_dim(column_ends, blk_index, 0, keepdims=False)
    blank_ends = jnp.zeros((2 * TILES_DEV, stack_rows, BS), stacked.dtype)
    shard_piece = lax.all_gather(own_data, "blk", axis=0, tiled=True)
    inside = jnp.logical_and(my_ends >= 0, my_ends < shard_piece.shape[0])
    picked = jnp.take(shard_piece, jnp.clip(my_ends, 0, shard_piece.shape[0] - 1), axis=0)
    ends_data = jnp.where(inside[:, None, None], picked, blank_ends)

    def one_tile(ends_pair):
        return tile_response(ends_pair[0], ends_pair[1], inv_scale, feature_count)

    responses = lax.map(one_tile, (ends_data[:TILES_DEV], ends_data[TILES_DEV:]))
    row_cap = (TILES_DEV + n_blk - 1) // n_blk
    row_holders = my_ends[:TILES_DEV] // owned_blocks
    row_ranks = rank_among(row_holders)
    targets = row_holders * row_cap + row_ranks
    slot_hit = targets[None, :] == jnp.arange(n_blk * row_cap, dtype=jnp.int32)[:, None]
    tile_pick = jnp.sum(
        jnp.where(slot_hit, jnp.arange(TILES_DEV, dtype=jnp.int32)[None, :], 0), axis=1
    )
    present = jnp.any(slot_hit, axis=1)
    outbound = jnp.where(present[:, None, None], jnp.take(responses, tile_pick, axis=0), 0.0)
    outbound = outbound.reshape(n_blk, row_cap, responses.shape[1], BS)
    returned = lax.all_to_all(outbound, "blk", split_axis=0, concat_axis=0, tiled=True)
    all_row_holders = column_rows // owned_blocks
    all_row_ranks = rank_among(all_row_holders)
    row_slots = lax.broadcasted_iota(jnp.int32, (n_blk, row_cap, TILES_DEV), 1)
    row_matched = jnp.logical_and(
        all_row_holders[:, None, :] == blk_index, all_row_ranks[:, None, :] == row_slots
    )
    target_block = jnp.sum(
        jnp.where(row_matched, (column_rows - blk_index * owned_blocks)[:, None, :], 0), axis=2
    )
    is_live = jnp.any(row_matched, axis=2)
    selected = jnp.logical_and(
        target_block[:, :, None] == jnp.arange(owned_blocks, dtype=jnp.int32), is_live[:, :, None]
    )
    gathered_terms = jnp.where(selected[:, :, :, None, None], returned[:, :, None, :, :], 0.0)
    partial_value = jnp.sum(gathered_terms, axis=(0, 1))
    partial_value = jnp.transpose(partial_value, (1, 0, 2)).reshape(
        responses.shape[1], owned_blocks * BS
    )
    return lax.psum_scatter(partial_value, "sub", scatter_dimension=1, tiled=True)


def solution(mesh):
    return jax.shard_map(
        per_device,
        mesh=mesh,
        in_specs=(P(None, "blk"), P(None, "blk"), P(), P(), P()),
        out_specs=P(None, ("blk", "sub")),
        check_vma=False,
    )
```

profile of v0, /device:TPU:28, one launch (start us, length us, event | category | flops | bytes accessed | tf_op | source)
XLA Modules:
  0.0 387.9 jit_solution(10094495012670031505)
XLA Ops:
  12.0 120.5 %all-gather.2.cloned.1.call-done = bf16[512,24,1024]{2,1,0:T(8,128)(2,1)} async-done(((bf16[8,24,1024]{2,1,0:T(8,128)(2,1)}), bf16[512,24,1024]{2,1,0:T(8,128)(2,1)}) %all-gather.2.cloned.1.call-update) | async-done | bytes 25165840 | tf_op jit(solution)/shard_map/all_gather | solution.py:64
  132.5 8.9 %gather_fusion = bf16[64,24,1024]{2,1,0:T(8,128)(2,1)S(1)} fusion(bf16[512,24,1024]{2,1,0:T(8,128)(2,1)} %all-gather.2.cloned.1.call-done, s32[1024]{0:T(1024)S(1)} %pad_clamp_fusion.1), kind=kCustom, calls=%fused_computation | custom fusion | bytes 6291712 | tf_op jit(solution)/shard_map/jit(_take)/gather | solution.py:66
  143.4 155.8 %while.10 = (s32[]{:T(128)}, f32[32,8,1024]{2,1,0:T(8,128)S(1)}, bf16[32,24,1024]{2,1,0:T(8,128)(2,1)}, f32[16]{0:T(128)S(1)}, bf16[32,24,1024]{2,1,0:T(8,128)(2,1)S(1)}, /*index=5*/s32[]{:T(128)}, s32[]{:T(128)}, s32[]{}) while((s32[]{:T(128)}, f32[32,8,1024]{2,1,0:T(8,128)S(1)}, bf16[32,24,1024]{2,1,0:T(8,128)(2,1)}, f32[16]{0:T(128)S(1)}, ...), condition=%wide.region_9.10_spmd, body=%wide.region_6.9_spmd.sunk | while | flops 66254848 | bytes 329389 | solution.py:72
  149.1 4.0 %fusion.31 = f32[32,8,1024]{2,1,0:T(8,128)S(1)} fusion(f32[32,8,1024]{2,1,0:T(8,128)S(1)} %get-tuple-element.104, s32[]{:T(128)S(6)} %copy.33, bf16[16,1024]{1,0:T(8,128)(2,1)S(1)} %get-tuple-element.91, bf16[16,1024]{1,0:T(8,128)(2,1)S(1)} %get-tuple-element.92, f32[1024]{0:T(1024)S(1)} %get-tuple-element.93, f32[1024]{0:T(1024)S(1)} %get-tuple-element.94, ...), kind=kOutput, calls=%fused_computation.5.clone.1 | convolution fusion | flops 66060288 | bytes 124416 | tf_op jit(solution)/shard_map/while/body/eval_jaxpr/dot_general | solution.py:33
  154.0 4.0 %fusion.31 = f32[32,8,1024]{2,1,0:T(8,128)S(1)} fusion(f32[32,8,1024]{2,1,0:T(8,128)S(1)} %get-tuple-element.104, s32[]{:T(128)S(6)} %copy.33, bf16[16,1024]{1,0:T(8,128)(2,1)S(1)} %get-tuple-element.91, bf16[16,1024]{1,0:T(8,128)(2,1)S(1)} %get-tuple-element.92, f32[1024]{0:T(1024)S(1)} %get-tuple-element.93, f32[1024]{0:T(1024)S(1)} %get-tuple-element.94, ...), kind=kOutput, calls=%fused_computation.5.clone.1 | convolution fusion | flops 66060288 | bytes 124416 | tf_op jit(solution)/shard_map/while/body/eval_jaxpr/dot_general | solution.py:33
  163.7 4.0 %fusion.31 = f32[32,8,1024]{2,1,0:T(8,128)S(1)} fusion(f32[32,8,1024]{2,1,0:T(8,128)S(1)} %get-tuple-element.104, s32[]{:T(128)S(6)} %copy.33, bf16[16,1024]{1,0:T(8,128)(2,1)S(1)} %get-tuple-element.91, bf16[16,1024]{1,0:T(8,128)(2,1)S(1)} %get-tuple-element.92, f32[1024]{0:T(1024)S(1)} %get-tuple-element.93, f32[1024]{0:T(1024)S(1)} %get-tuple-element.94, ...), kind=kOutput, calls=%fused_computation.5.clone.1 | convolution fusion | flops 66060288 | bytes 124416 | tf_op jit(solution)/shard_map/while/body/eval_jaxpr/dot_general | solution.py:33
  168.6 4.0 %fusion.31 = f32[32,8,1024]{2,1,0:T(8,128)S(1)} fusion(f32[32,8,1024]{2,1,0:T(8,128)S(1)} %get-tuple-element.104, s32[]{:T(128)S(6)} %copy.33, bf16[16,1024]{1,0:T(8,128)(2,1)S(1)} %get-tuple-element.91, bf16[16,1024]{1,0:T(8,128)(2,1)S(1)} %get-tuple-element.92, f32[1024]{0:T(1024)S(1)} %get-tuple-element.93, f32[1024]{0:T(1024)S(1)} %get-tuple-element.94, ...), kind=kOutput, calls=%fused_computation.5.clone.1 | convolution fusion | flops 66060288 | bytes 124416 | tf_op jit(solution)/shard_map/while/body/eval_jaxpr/dot_general | solution.py:33
  178.4 4.0 %fusion.31 = f32[32,8,1024]{2,1,0:T(8,128)S(1)} fusion(f32[32,8,1024]{2,1,0:T(8,128)S(1)} %get-tuple-element.104, s32[]{:T(128)S(6)} %copy.33, bf16[16,1024]{1,0:T(8,128)(2,1)S(1)} %get-tuple-element.91, bf16[16,1024]{1,0:T(8,128)(2,1)S(1)} %get-tuple-element.92, f32[1024]{0:T(1024)S(1)} %get-tuple-element.93, f32[1024]{0:T(1024)S(1)} %get-tuple-element.94, ...), kind=kOutput, calls=%fused_computation.5.clone.1 | convolution fusion | flops 66060288 | bytes 124416 | tf_op jit(solution)/shard_map/while/body/eval_jaxpr/dot_general | solution.py:33
  183.2 4.0 %fusion.31 = f32[32,8,1024]{2,1,0:T(8,128)S(1)} fusion(f32[32,8,1024]{2,1,0:T(8,128)S(1)} %get-tuple-element.104, s32[]{:T(128)S(6)} %copy.33, bf16[16,1024]{1,0:T(8,128)(2,1)S(1)} %get-tuple-element.91, bf16[16,1024]{1,0:T(8,128)(2,1)S(1)} %get-tuple-element.92, f32[1024]{0:T(1024)S(1)} %get-tuple-element.93, f32[1024]{0:T(1024)S(1)} %get-tuple-element.94, ...), kind=kOutput, calls=%fused_computation.5.clone.1 | convolution fusion | flops 66060288 | bytes 124416 | tf_op jit(solution)/shard_map/while/body/eval_jaxpr/dot_general | solution.py:33
  193.0 4.0 %fusion.31 = f32[32,8,1024]{2,1,0:T(8,128)S(1)} fusion(f32[32,8,1024]{2,1,0:T(8,128)S(1)} %get-tuple-element.104, s32[]{:T(128)S(6)} %copy.33, bf16[16,1024]{1,0:T(8,128)(2,1)S(1)} %get-tuple-element.91, bf16[16,1024]{1,0:T(8,128)(2,1)S(1)} %get-tuple-element.92, f32[1024]{0:T(1024)S(1)} %get-tuple-element.93, f32[1024]{0:T(1024)S(1)} %get-tuple-element.94, ...), kind=kOutput, calls=%fused_computation.5.clone.1 | convolution fusion | flops 66060288 | bytes 124416 | tf_op jit(solution)/shard_map/while/body/eval_jaxpr/dot_general | solution.py:33
  197.8 4.0 %fusion.31 = f32[32,8,1024]{2,1,0:T(8,128)S(1)} fusion(f32[32,8,1024]{2,1,0:T(8,128)S(1)} %get-tuple-element.104, s32[]{:T(128)S(6)} %copy.33, bf16[16,1024]{1,0:T(8,128)(2,1)S(1)} %get-tuple-element.91, bf16[16,1024]{1,0:T(8,128)(2,1)S(1)} %get-tuple-element.92, f32[1024]{0:T(1024)S(1)} %get-tuple-element.93, f32[1024]{0:T(1024)S(1)} %get-tuple-element.94, ...), kind=kOutput, calls=%fused_computation.5.clone.1 | convolution fusion | flops 66060288 | bytes 124416 | tf_op jit(solution)/shard_map/while/body/eval_jaxpr/dot_general | solution.py:33
  207.6 4.0 %fusion.31 = f32[32,8,1024]{2,1,0:T(8,128)S(1)} fusion(f32[32,8,1024]{2,1,0:T(8,128)S(1)} %get-tuple-element.104, s32[]{:T(128)S(6)} %copy.33, bf16[16,1024]{1,0:T(8,128)(2,1)S(1)} %get-tuple-element.91, bf16[16,1024]{1,0:T(8,128)(2,1)S(1)} %get-tuple-element.92, f32[1024]{0:T(1024)S(1)} %get-tuple-element.93, f32[1024]{0:T(1024)S(1)} %get-tuple-element.94, ...), kind=kOutput, calls=%fused_computation.5.clone.1 | convolution fusion | flops 66060288 | bytes 124416 | tf_op jit(solution)/shard_map/while/body/eval_jaxpr/dot_general | solution.py:33
  212.5 4.0 %fusion.31 = f32[32,8,1024]{2,1,0:T(8,128)S(1)} fusion(f32[32,8,1024]{2,1,0:T(8,128)S(1)} %get-tuple-element.104, s32[]{:T(128)S(6)} %copy.33, bf16[16,1024]{1,0:T(8,128)(2,1)S(1)} %get-tuple-element.91, bf16[16,1024]{1,0:T(8,128)(2,1)S(1)} %get-tuple-element.92, f32[1024]{0:T(1024)S(1)} %get-tuple-element.93, f32[1024]{0:T(1024)S(1)} %get-tuple-element.94, ...), kind=kOutput, calls=%fused_computation.5.clone.1 | convolution fusion | flops 66060288 | bytes 124416 | tf_op jit(solution)/shard_map/while/body/eval_jaxpr/dot_general | solution.py:33
  222.2 4.0 %fusion.31 = f32[32,8,1024]{2,1,0:T(8,128)S(1)} fusion(f32[32,8,1024]{2,1,0:T(8,128)S(1)} %get-tuple-element.104, s32[]{:T(128)S(6)} %copy.33, bf16[16,1024]{1,0:T(8,128)(2,1)S(1)} %get-tuple-element.91, bf16[16,1024]{1,0:T(8,128)(2,1)S(1)} %get-tuple-element.92, f32[1024]{0:T(1024)S(1)} %get-tuple-element.93, f32[1024]{0:T(1024)S(1)} %get-tuple-element.94, ...), kind=kOutput, calls=%fused_computation.5.clone.1 | convolution fusion | flops 66060288 | bytes 124416 | tf_op jit(solution)/shard_map/while/body/eval_jaxpr/dot_general | solution.py:33
  227.1 4.0 %fusion.31 = f32[32,8,1024]{2,1,0:T(8,128)S(1)} fusion(f32[32,8,1024]{2,1,0:T(8,128)S(1)} %get-tuple-element.104, s32[]{:T(128)S(6)} %copy.33, bf16[16,1024]{1,0:T(8,128)(2,1)S(1)} %get-tuple-element.91, bf16[16,1024]{1,0:T(8,128)(2,1)S(1)} %get-tuple-element.92, f32[1024]{0:T(1024)S(1)} %get-tuple-element.93, f32[1024]{0:T(1024)S(1)} %get-tuple-element.94, ...), kind=kOutput, calls=%fused_computation.5.clone.1 | convolution fusion | flops 66060288 | bytes 124416 | tf_op jit(solution)/shard_map/while/body/eval_jaxpr/dot_general | solution.py:33
  236.8 4.0 %fusion.31 = f32[32,8,1024]{2,1,0:T(8,128)S(1)} fusion(f32[32,8,1024]{2,1,0:T(8,128)S(1)} %get-tuple-element.104, s32[]{:T(128)S(6)} %copy.33, bf16[16,1024]{1,0:T(8,128)(2,1)S(1)} %get-tuple-element.91, bf16[16,1024]{1,0:T(8,128)(2,1)S(1)} %get-tuple-element.92, f32[1024]{0:T(1024)S(1)} %get-tuple-element.93, f32[1024]{0:T(1024)S(1)} %get-tuple-element.94, ...), kind=kOutput, calls=%fused_computation.5.clone.1 | convolution fusion | flops 66060288 | bytes 124416 | tf_op jit(solution)/shard_map/while/body/eval_jaxpr/dot_general | solution.py:33
  251.4 4.0 %fusion.31 = f32[32,8,1024]{2,1,0:T(8,128)S(1)} fusion(f32[32,8,1024]{2,1,0:T(8,128)S(1)} %get-tuple-element.104, s32[]{:T(128)S(6)} %copy.33, bf16[16,1024]{1,0:T(8,128)(2,1)S(1)} %get-tuple-element.91, bf16[16,1024]{1,0:T(8,128)(2,1)S(1)} %get-tuple-element.92, f32[1024]{0:T(1024)S(1)} %get-tuple-element.93, f32[1024]{0:T(1024)S(1)} %get-tuple-element.94, ...), kind=kOutput, calls=%fused_computation.5.clone.1 | convolution fusion | flops 66060288 | bytes 124416 | tf_op jit(solution)/shard_map/while/body/eval_jaxpr/dot_general | solution.py:33
  256.3 4.0 %fusion.31 = f32[32,8,1024]{2,1,0:T(8,128)S(1)} fusion(f32[32,8,1024]{2,1,0:T(8,128)S(1)} %get-tuple-element.104, s32[]{:T(128)S(6)} %copy.33, bf16[16,1024]{1,0:T(8,128)(2,1)S(1)} %get-tuple-element.91, bf16[16,1024]{1,0:T(8,128)(2,1)S(1)} %get-tuple-element.92, f32[1024]{0:T(1024)S(1)} %get-tuple-element.93, f32[1024]{0:T(1024)S(1)} %get-tuple-element.94, ...), kind=kOutput, calls=%fused_computation.5.clone.1 | convolution fusion | flops 66060288 | bytes 124416 | tf_op jit(solution)/shard_map/while/body/eval_jaxpr/dot_general | solution.py:33
  266.0 4.0 %fusion.31 = f32[32,8,1024]{2,1,0:T(8,128)S(1)} fusion(f32[32,8,1024]{2,1,0:T(8,128)S(1)} %get-tuple-element.104, s32[]{:T(128)S(6)} %copy.33, bf16[16,1024]{1,0:T(8,128)(2,1)S(1)} %get-tuple-element.91, bf16[16,1024]{1,0:T(8,128)(2,1)S(1)} %get-tuple-element.92, f32[1024]{0:T(1024)S(1)} %get-tuple-element.93, f32[1024]{0:T(1024)S(1)} %get-tuple-element.94, ...), kind=kOutput, calls=%fused_computation.5.clone.1 | convolution fusion | flops 66060288 | bytes 124416 | tf_op jit(solution)/shard_map/while/body/eval_jaxpr/dot_general | solution.py:33
  280.6 4.0 %fusion.31 = f32[32,8,1024]{2,1,0:T(8,128)S(1)} fusion(f32[32,8,1024]{2,1,0:T(8,128)S(1)} %get-tuple-element.104, s32[]{:T(128)S(6)} %copy.33, bf16[16,1024]{1,0:T(8,128)(2,1)S(1)} %get-tuple-element.91, bf16[16,1024]{1,0:T(8,128)(2,1)S(1)} %get-tuple-element.92, f32[1024]{0:T(1024)S(1)} %get-tuple-element.93, f32[1024]{0:T(1024)S(1)} %get-tuple-element.94, ...), kind=kOutput, calls=%fused_computation.5.clone.1 | convolution fusion | flops 66060288 | bytes 124416 | tf_op jit(solution)/shard_map/while/body/eval_jaxpr/dot_general | solution.py:33
  295.2 4.0 %fusion.31 = f32[32,8,1024]{2,1,0:T(8,128)S(1)} fusion(f32[32,8,1024]{2,1,0:T(8,128)S(1)} %get-tuple-element.104, s32[]{:T(128)S(6)} %copy.33, bf16[16,1024]{1,0:T(8,128)(2,1)S(1)} %get-tuple-element.91, bf16[16,1024]{1,0:T(8,128)(2,1)S(1)} %get-tuple-element.92, f32[1024]{0:T(1024)S(1)} %get-tuple-element.93, f32[1024]{0:T(1024)S(1)} %get-tuple-element.94, ...), kind=kOutput, calls=%fused_computation.5.clone.1 | convolution fusion | flops 66060288 | bytes 124416 | tf_op jit(solution)/shard_map/while/body/eval_jaxpr/dot_general | solution.py:33
  301.6 8.1 %all-to-all-start = ((f32[64,1,8,1024]{3,2,1,0:T(8,128)}), f32[64,1,8,1024]{3,2,1,0:T(8,128)S(1)}, u32[]{:S(2)}, u32[]{:S(2)}) async-start(f32[64,1,8,1024]{3,2,1,0:T(8,128)} %fusion.10), calls=%async_computation | async-start | bytes 4194304 | tf_op jit(solution)/shard_map/all_to_all | solution.py:84
  312.8 45.5 %all-to-all-done = f32[64,1,8,1024]{3,2,1,0:T(8,128)S(1)} async-done(((f32[64,1,8,1024]{3,2,1,0:T(8,128)}), f32[64,1,8,1024]{3,2,1,0:T(8,128)S(1)}, u32[]{:S(2)}, u32[]{:S(2)}) %all-to-all-start) | async-done | bytes 2097184 | tf_op jit(solution)/shard_map/all_to_all | solution.py:84
  360.5 20.5 %reduce-scatter.2.cloned.1.call-done = f32[8,2048]{1,0:T(8,128)} async-done(((f32[8,8192]{1,0:T(8,128)}), f32[8,2048]{1,0:T(8,128)}) %reduce-scatter.2.cloned.1.call-update) | async-done | bytes 65552 | tf_op jit(solution)/shard_map/reduce_scatter | solution.py:103
  (124 shorter events, 98.7 us)
Async XLA Ops:
  6.5 126.0 %all-gather.2.cloned.1.call-start = ((), (), s32[]{:S(2)}) async-start(), calls=%async_computation.2 | async-start | bytes 25559040 | tf_op jit(solution)/shard_map/all_gather | solution.py:64
  141.9 1.5 copy-start
  141.9 1.5 copy-start.1
  301.6 56.7 %all-to-all-start = ((f32[64,1,8,1024]{3,2,1,0:T(8,128)}), f32[64,1,8,1024]{3,2,1,0:T(8,128)S(1)}, u32[]{:S(2)}, u32[]{:S(2)}) async-start(f32[64,1,8,1024]{3,2,1,0:T(8,128)} %fusion.10), calls=%async_computation | async-start | bytes 4194304 | tf_op jit(solution)/shard_map/all_to_all | solution.py:84
  309.6 71.4 %reduce-scatter.2.cloned.1.call-start = ((), (), s32[]{:S(2)}) async-start(), calls=%async_computation.3 | async-start | bytes 327680 | tf_op jit(solution)/shard_map/reduce_scatter | solution.py:103
Sparse Core Ops, SparseCore 0:
  10.1 122.3 all-gather.1
  360.6 20.3 reduce-scatter.1
where the time goes:
time: 394 us; the launch traced here: 388 us
  waiting for transfers between devices  187 us (47%)
  matrix products  128 us (32%)
  other arithmetic  37.2 us (9%)
  local copies, waits for them, and re-layouts  14.4 us (4%)
  between operations  13.6 us (3%)
  starting transfers between devices  8.1 us (2%)
    dot_general x32, matrix products, tile_response(): jnp.dot(col_data[feature_count:], kernel, preferred_element_type=jnp.floa...  128 us
    all_gather x1, waiting for transfers between devices, per_device(): shard_piece = lax.all_gather(own_data, 'blk', axis=0, tiled=True)  121 us
    all_to_all x1, waiting for transfers between devices, per_device(): lax.all_to_all(outbound, 'blk', split_axis=0, concat_axis=0, tiled=True)  45.5 us
    convert_element_type x32, other arithmetic, scale_rows(): (data[:feature_count].astype(jnp.float32) * inv_scale[:, None]).astype(jn...  26.9 us
    reduce_scatter x1, waiting for transfers between devices, per_device(): lax.psum_scatter(partial_value, 'sub', scatter_dimension=1, tiled=True)  20.5 us
    gather x1, local copies, waits for them, and re-layouts, per_device(): jnp.take(shard_piece, jnp.clip(my_ends, 0, shard_piece.shape[0] - 1), axi...  8.9 us
    all_to_all x1, starting transfers between devices, per_device(): lax.all_to_all(outbound, 'blk', split_axis=0, concat_axis=0, tiled=True)  8.06 us
  transfers between devices with their start and end apart: 3, of which 3 were waited for; matrix products, arithmetic and copies ran while one was open for 2% of the time, Pallas kernels for 0%

commit v1 on v0

v1 whole, which is shorter than its diff:
```python
import functools

import jax
import jax.numpy as jnp
from jax import lax
from jax.experimental import pallas as pl
from jax.experimental.pallas import tpu as pltpu
from jax.sharding import PartitionSpec as P

BS = 1024
TILES = 32
B_DEV = 8
NX, NZ, NY = 4, 8, 4
PLANE = NX * NY * 2
PROBES = 8
CHUNKS = 2
N = BS // CHUNKS
HALF = N // 2
W = N + HALF
KP = 32
SUBC = 256
PLAN = (
    (((0, 512, 0, 512), None),),
    (((0, 512, 512, 512), 0), ((512, 512, 0, 1024), 1)),
)
RETURNS = ((0, 512), (512, 512))
MESH = pl.DeviceIdType.MESH
F32 = jnp.float32
BF16 = jnp.bfloat16
SEL, RSEL, ROW_SLOT, COL_SLOT, TILE_OF = 0, 64, 128, 160, 192


def wendland11(sq_dist):
    s = jnp.minimum(jnp.maximum(sq_dist, 1e-30), 1.0)
    remain = 1.0 - s * lax.rsqrt(s)
    square = remain * remain
    fourth = square * square
    eighth = fourth * fourth
    return ((eighth * square) * (remain * (12.0 / 11.0 - remain))).astype(BF16)


def place(blk, sub):
    return blk // (2 * NZ), (blk // 2) % NZ, sub, blk % 2


def sources_of(z, y):
    k = lax.rem(z - y + NZ, 4)
    z_up = jnp.where(k > 0, lax.rem(z - k + NZ, NZ), lax.rem(z + 4, NZ))
    z_down = jnp.where(k > 0, lax.rem(z + 4 - k, NZ), z)
    return k, z_up, z_down


def tables(tile_rows, tile_cols):
    x, z, y, c = place(lax.axis_index("blk"), lax.axis_index("sub"))
    _, z_up, z_down = sources_of(z, y)

    def in_plane(tiles):
        tiles = tiles.reshape(NX, NZ, 2, NY, TILES)
        tiles = lax.dynamic_index_in_dim(tiles, z, 1, keepdims=False)
        return tiles.transpose(0, 2, 1, 3).reshape(PLANE, TILES)

    rows, cols = in_plane(tile_rows), in_plane(tile_cols)
    ends = jnp.concatenate([rows, cols], axis=1)
    owned = jnp.stack([(x * NZ + z_up) * 2 + c, (x * NZ + z_down) * 2 + c])
    sel = jnp.sum(
        jnp.where((ends // B_DEV)[:, None, :] == owned[None, :, None], (ends % B_DEV)[:, None, :], 0), axis=2
    )
    rsel = jnp.sum(
        jnp.where((rows // B_DEV)[:, None, :] == owned[None, :, None], (rows % B_DEV + 1)[:, None, :], 0), axis=2
    ) - 1
    mine = lax.dynamic_index_in_dim(ends, (x * NY + y) * 2 + c, 0, keepdims=False)
    owner = mine // B_DEV
    ox, oz, oc = owner // (2 * NZ), (owner // 2) % NZ, owner % 2
    oy = oz % NY
    _, o_up, _ = sources_of(z, oy)
    slot = ((ox * NY + oy) * 2 + oc) * 2 + jnp.where(oz == o_up, 0, 1)
    row_slot = slot[:TILES]
    hit = row_slot[None, :] == jnp.arange(2 * PLANE, dtype=jnp.int32)[:, None]
    tile_of = jnp.min(jnp.where(hit, jnp.arange(TILES, dtype=jnp.int32)[None, :], TILES), axis=1)
    return jnp.concatenate([sel.reshape(-1), rsel.reshape(-1), slot, tile_of]).astype(jnp.int32)


def kernel(feat, prob, inv, tab, out, *scratch):
    it = iter(scratch)
    down = [next(it) for _ in range(CHUNKS)]
    up = [next(it) for _ in range(CHUNKS)]
    sbuf = [next(it) for _ in range(CHUNKS)]
    rbuf = [next(it) for _ in range(CHUNKS)]
    s1 = [next(it) for _ in RETURNS]
    r1 = [next(it) for _ in RETURNS]
    s2 = [next(it) for _ in RETURNS]
    r2 = [next(it) for _ in RETURNS]
    rowm, colm, pr, res = next(it), next(it), next(it), next(it)
    up_send, up_recv, down_send, down_recv, a_send, a_recv = [next(it) for _ in range(6)]
    b_send, b_recv, c_send, c_recv = [next(it) for _ in range(4)]

    blk, sub = lax.axis_index("blk"), lax.axis_index("sub")
    x, z, y, c = place(blk, sub)
    me = (x * NY + y) * 2 + c
    k, z_up, z_down = sources_of(z, y)
    is_source = k == 0

    def plane_peer(d):
        px, py, pc = lax.rem(x + d // 8, NX), lax.rem(y + (d // 2) % 4, NY), lax.rem(c + d % 2, 2)
        return (px * NZ + z) * 2 + pc, py, (px * NY + py) * 2 + pc

    def column(zz):
        return (x * NZ + zz) * 2 + c

    barrier = pltpu.get_barrier_semaphore()

    def greet(d, _):
        b, s, _p = plane_peer(d)
        pl.semaphore_signal(barrier, inc=1, device_id=(b, s), device_id_type=MESH)
        return 0

    lax.fori_loop(1, PLANE, greet, 0)
    for step in (1, NZ - 1):
        pl.semaphore_signal(barrier, inc=1, device_id=(column(lax.rem(z + step, NZ)), y), device_id_type=MESH)
    for zz in range(NZ):
        @pl.when(jnp.logical_or(jnp.logical_not(is_source), z != zz))
        def _():
            pl.semaphore_signal(
                barrier, inc=1, device_id=(column(zz), lax.rem(z, NY)), device_id_type=MESH
            )

    @pl.when(is_source)
    def _():
        scale = inv[...]
        for q in range(CHUNKS):
            for b in range(B_DEV):
                at = b * BS + q * N
                down[q][b, :, 0:N] = (feat[:, at:at + N].astype(F32) * scale).astype(BF16)
                p = prob[:, at:at + N].astype(F32)
                down[q][b, :, N:W] = jnp.concatenate([p[:, :HALF], p[:, HALF:]], axis=0).astype(BF16)

    @pl.when(is_source)
    def _():
        pl.semaphore_wait(barrier, PLANE - 1 + 2 + NZ - 1)

    @pl.when(jnp.logical_not(is_source))
    def _():
        pl.semaphore_wait(barrier, PLANE - 1 + 2 + NZ)

    def send_up(q, src):
        return pltpu.make_async_remote_copy(
            src_ref=src, dst_ref=up[q], send_sem=up_send.at[q], recv_sem=up_recv.at[q],
            device_id=(column(lax.rem(z + 1, NZ)), y), device_id_type=MESH)

    def send_down(q):
        return pltpu.make_async_remote_copy(
            src_ref=down[q], dst_ref=down[q], send_sem=down_send.at[q], recv_sem=down_recv.at[q],
            device_id=(column(lax.rem(z + NZ - 1, NZ)), y), device_id_type=MESH)

    def to_peer(q, d):
        b, s, _p = plane_peer(d)
        return pltpu.make_async_remote_copy(
            src_ref=sbuf[q].at[pl.ds(2 * d, 2)], dst_ref=rbuf[q].at[pl.ds(2 * me, 2)],
            send_sem=a_send.at[q], recv_sem=a_recv.at[q], device_id=(b, s), device_id_type=MESH)

    @pl.when(is_source)
    def _():
        for q in range(CHUNKS):
            send_up(q, down[q]).start()
            send_down(q).start()

    for q in range(CHUNKS):
        send_up(q, up[q]).wait_recv()

        @pl.when(jnp.logical_not(is_source))
        def _():
            send_up(q, up[q]).start()
            send_down(q).wait_recv()

        @pl.when(k >= 2)
        def _():
            send_down(q).start()

        rbuf[q][2 * me] = up[q][tab[SEL + 2 * me]]
        rbuf[q][2 * me + 1] = down[q][tab[SEL + 2 * me + 1]]

        def pick(d, _):
            _b, _s, p = plane_peer(d)
            sbuf[q][2 * d] = up[q][tab[SEL + 2 * p]]
            sbuf[q][2 * d + 1] = down[q][tab[SEL + 2 * p + 1]]
            to_peer(q, d).start()
            return 0

        lax.fori_loop(1, PLANE, pick, 0)

    res[TILES] = jnp.zeros((PROBES, BS), F32)

    def all_but_one(ref):
        size = ref.shape[0] // PLANE * (PLANE - 1)
        return ref.at[pl.ds(0, size)]

    def prepare(q):
        at = q * N
        line = lax.broadcasted_iota(jnp.int32, (8, N), 0)

        def one(t, _):
            def parts(g):
                g = g.astype(F32)
                sq = jnp.sum(g * g, axis=0, keepdims=True)
                hi = sq.astype(BF16).astype(F32)
                mid = (sq - hi).astype(BF16).astype(F32)
                low = (sq - hi) - mid
                split = jnp.where(line == 0, hi, jnp.where(line == 1, mid, jnp.where(line == 2, low, 0.0)))
                ones = jnp.where(line < 3, 1.0, 0.0)
                return g, split, ones

            g, split, ones = parts(rbuf[q][tab[ROW_SLOT + t], :, 0:N])
            rowm[t, :, at:at + N] = jnp.concatenate([-2.0 * g, split, ones], axis=0).astype(BF16)
            both = rbuf[q][tab[COL_SLOT + t]]
            g, split, ones = parts(both[:, 0:N])
            colm[t, at:at + N, :] = jnp.swapaxes(jnp.concatenate([g, ones, split], axis=0), 0, 1).astype(BF16)
            p = both[:, N:W].astype(F32)
            pr[t, :, at:at + N] = jnp.concatenate([p[0:8], p[8:16]], axis=1).astype(BF16)
            return 0

        lax.fori_loop(0, TILES, one, 0)

    def compute(r0, rn, c0, cn):
        def one(t, _):
            row = rowm[t, :, r0:r0 + rn]
            tiles = [
                wendland11(jnp.dot(colm[t, j:j + SUBC, :], row, preferred_element_type=F32))
                for j in range(c0, c0 + cn, SUBC)
            ]
            part = jnp.dot(pr[t, :, c0:c0 + cn], jnp.concatenate(tiles, axis=0), preferred_element_type=F32)
            if c0 > 0:
                part = part + res[t, :, r0:r0 + rn]
            res[t, :, r0:r0 + rn] = part
            return 0

        lax.fori_loop(0, TILES, one, 0)

    def give_back(a):
        r0, rn = RETURNS[a]

        def copy(d):
            b, s, _p = plane_peer(d)
            return pltpu.make_async_remote_copy(
                src_ref=s1[a].at[d], dst_ref=r1[a].at[me], send_sem=b_send.at[a], recv_sem=b_recv.at[a],
                device_id=(b, s), device_id_type=MESH)

        def packed(p):
            both = [res[tab[TILE_OF + 2 * p + h], :, r0:r0 + rn] * 11.0 for h in range(2)]
            return jnp.concatenate(both, axis=0).astype(BF16)

        r1[a][me] = packed(me)

        def one(d, _):
            _b, _s, p = plane_peer(d)
            s1[a][d] = packed(p)
            copy(d).start()
            return 0

        lax.fori_loop(1, PLANE, one, 0)

    def second(a, h, s, zz):
        return pltpu.make_async_remote_copy(
            src_ref=s2[a].at[h, s], dst_ref=r2[a].at[z], send_sem=c_send.at[a], recv_sem=c_recv.at[a],
            device_id=(column(zz), s), device_id_type=MESH)

    def add_up(a):
        r0, rn = RETURNS[a]
        land = all_but_one(r1[a])
        pltpu.make_async_copy(land, land, b_recv.at[a]).wait()
        step = min(rn, 256)
        for w in range(0, rn, step):
            def one(p, sums):
                got = r1[a][p, :, w:w + step].astype(F32)
                new = []
                for h in range(2):
                    which = tab[RSEL + 2 * p + h]
                    term = got[8 * h:8 * h + 8]
                    for b in range(B_DEV):
                        new.append(sums[h * B_DEV + b] + jnp.where(which == b, term, 0.0))
                return tuple(new)

            zero = jnp.zeros((PROBES, step), F32)
            sums = lax.fori_loop(0, PLANE, one, (zero,) * (2 * B_DEV))
            for h in range(2):
                for b in range(B_DEV):
                    s2[a][h, b // 2, b % 2, :, w:w + step] = sums[h * B_DEV + b]
        for h, zz in ((0, z_up), (1, z_down)):
            for s in range(NY):
                if h == 1:
                    own = jnp.logical_and(is_source, y == s)

                    @pl.when(own)
                    def _():
                        r2[a][z] = s2[a][h, s]

                    @pl.when(jnp.logical_not(own))
                    def _():
                        second(a, h, s, zz).start()
                else:
                    second(a, h, s, zz).start()

    def finish(a):
        r0, rn = RETURNS[a]

        @pl.when(is_source)
        def _():
            land = r2[a].at[pl.ds(0, NZ - 1)]
            pltpu.make_async_copy(land, land, c_recv.at[a]).wait()

        @pl.when(jnp.logical_not(is_source))
        def _():
            pltpu.make_async_copy(r2[a], r2[a], c_recv.at[a]).wait()

        for b in range(2):
            total = r2[a][0, b]
            for zz in range(1, NZ):
                total = total + r2[a][zz, b]
            out[:, b * BS + r0:b * BS + r0 + rn] = total

    for q in range(CHUNKS):
        land = all_but_one(rbuf[q])
        pltpu.make_async_copy(land, land, a_recv.at[q]).wait()
        prepare(q)
        for rect, back in PLAN[q]:
            compute(*rect)
            if back is not None:
                give_back(back)
    for a in range(len(RETURNS)):
        add_up(a)
    for a in range(len(RETURNS)):
        finish(a)

    for q in range(CHUNKS):
        send_up(q, up[q]).wait_send()

        @pl.when(k != 1)
        def _():
            send_down(q).wait_send()

        left = all_but_one(sbuf[q])
        pltpu.make_async_copy(left, left, a_send.at[q]).wait()
    for a in range(len(RETURNS)):
        left = all_but_one(s1[a])
        pltpu.make_async_copy(left, left, b_send.at[a]).wait()
        for h in range(2):
            for s in range(NY):
                @pl.when(jnp.logical_not(jnp.logical_and(is_source, jnp.logical_and(h == 1, y == s))))
                def _():
                    second(a, h, s, z).wait_send()


def per_device(features, probes, inv_scale, tile_rows, tile_cols):
    tab = tables(tile_rows, tile_cols)
    vmem, smem = pl.BlockSpec(memory_space=pltpu.VMEM), pl.BlockSpec(memory_space=pltpu.SMEM)
    nr = len(RETURNS)
    dma = pltpu.SemaphoreType.DMA
    scratch = (
        [pltpu.VMEM((B_DEV, 16, W), BF16)] * (2 * CHUNKS)
        + [pltpu.VMEM((2 * PLANE, 16, W), BF16)] * (2 * CHUNKS)
        + [pltpu.VMEM((PLANE, 16, rn), BF16) for _, rn in RETURNS] * 2
        + [pltpu.VMEM((2, NY, 2, PROBES, rn), F32) for _, rn in RETURNS]
        + [pltpu.VMEM((NZ, 2, PROBES, rn), F32) for _, rn in RETURNS]
        + [
            pltpu.VMEM((TILES, KP, BS), BF16),
            pltpu.VMEM((TILES, BS, KP), BF16),
            pltpu.VMEM((TILES, PROBES, BS), BF16),
            pltpu.VMEM((TILES + 1, PROBES, BS), F32),
        ]
        + [dma((CHUNKS,))] * 6
        + [dma((nr,))] * 4
    )
    return pl.pallas_call(
        kernel,
        out_shape=jax.ShapeDtypeStruct((PROBES, 2 * BS), F32),
        in_specs=[vmem, vmem, vmem, smem],
        out_specs=vmem,
        scratch_shapes=scratch,
        compiler_params=pltpu.CompilerParams(
            collective_id=0, has_side_effects=True, vmem_limit_bytes=56 * 1024 * 1024
        ),
    )(features, probes, inv_scale.reshape(-1, 1), tab)


def solution(mesh):
    return jax.shard_map(
        per_device,
        mesh=mesh,
        in_specs=(P(None, "blk"), P(None, "blk"), P(), P(), P()),
        out_specs=P(None, ("blk", "sub")),
        check_vma=False,
    )
```

time: 394 us -> 184 us (0.47); the launches traced: 388 us -> 184 us
  waiting for transfers between devices: 187 us -> 0 us
  Pallas kernels: 0 us -> 178 us
  matrix products: 128 us -> 0 us
  other arithmetic: 37.2 us -> 1.39 us
  between operations: 13.6 us -> 0.17 us
  local copies, waits for them, and re-layouts: 14.4 us -> 4.86 us
  starting transfers between devices: 8.1 us -> 0 us
    pallas_call x0 -> x1, Pallas kernels: none -> 178 us  [per_device(): pl.pallas_call(kernel, out_shape=jax.ShapeDtypeStruct((PROBES, 2 * BS), F...]
    dot_general x32 -> x0, matrix products: 128 us -> none  [tile_response(): jnp.dot(col_data[feature_count:], kernel, preferred_element_type=jnp.floa...]
    all_gather x1 -> x0, waiting for transfers between devices: 121 us -> none  [per_device(): shard_piece = lax.all_gather(own_data, 'blk', axis=0, tiled=True)]
    all_to_all x1 -> x0, waiting for transfers between devices: 45.5 us -> none  [per_device(): lax.all_to_all(outbound, 'blk', split_axis=0, concat_axis=0, tiled=True)]
    convert_element_type x32 -> x0, other arithmetic: 26.9 us -> none  [scale_rows(): (data[:feature_count].astype(jnp.float32) * inv_scale[:, None]).astype(jn...]
    reduce_scatter x1 -> x0, waiting for transfers between devices: 20.5 us -> none  [per_device(): lax.psum_scatter(partial_value, 'sub', scatter_dimension=1, tiled=True)]
    gather x2 -> x0, local copies, waits for them, and re-layouts: 9.59 us -> none  [the longest x1 8.9 us: per_device(): jnp.take(shard_piece, jnp.clip(my_ends, 0, shard_piece.shape[0] - 1), axi...]
    all_to_all x1 -> x0, starting transfers between devices: 8.06 us -> none  [per_device(): lax.all_to_all(outbound, 'blk', split_axis=0, concat_axis=0, tiled=True)]
  transfers between devices with their start and end apart: 3 -> 0, of which waited for: 3 -> 0; matrix products, arithmetic and copies ran while one was open for 2% -> 0% of each run, Pallas kernels for 0% -> 0%
where the time goes in v1:
time: 184 us
  Pallas kernels  178 us (97%)
  local copies, waits for them, and re-layouts  4.86 us (3%)
    pallas_call x1, Pallas kernels, per_device(): pl.pallas_call(kernel, out_shape=jax.ShapeDtypeStruct((PROBES, 2 * BS), F...  178 us

profile of v1, /device:TPU:28, one launch (start us, length us, event | category | flops | bytes accessed | tf_op | source)
XLA Modules:
  0.0 183.9 jit_solution(12234178213293752157)
XLA Ops:
  0.0 0.0 copy-start
  0.0 0.8 copy-done
  0.8 0.0 copy-start.1
  0.8 0.1 reshape.189
  0.9 0.6 copy-done.1
  1.5 0.1 reshape.190
  1.7 0.1 add_select_fusion.3
  1.9 0.1 pad_add_fusion.2
  1.9 0.2 select_reduce_fusion.1
  2.1 0.1 copy.14
  2.2 0.1 reshape.191
  2.4 0.2 select_reduce_fusion
  2.5 0.1 copy.15
  2.6 0.1 sub.66
  2.8 0.1 fusion.11
  2.9 0.1 select_reduce_fusion.2
  3.0 0.6 pad_add_fusion.1.tab
  3.6 0.0 copy-start.2
  3.6 0.7 copy-done.2
  4.3 0.7 copy.16.inv
  4.9 177.5 %shard_map.55 = f32[8,2048]{1,0:T(8,128)} custom-call(bf16[16,8192]{1,0:T(8,128)(2,1)} %feat.1, bf16[8,8192]{1,0:T(8,128)(2,1)} %prob.1, f32[16,1]{1,0:T(8,128)} %copy.16.inv, s32[256]{0:T(256)} %pad_add_fusion.1.tab), custom_call_target="tpu_custom_call" | custom-call | tf_op jit(solution)/shard_map/pallas_call | solution.py:372
  182.5 1.5 copy.18
  (5 shorter events, 0.1 us)
Async XLA Ops:
  0.0 0.8 copy-start
  0.8 0.8 copy-start.1
  3.6 0.7 copy-start.2

commit v2 on v1

--- a/solution.py
+++ b/solution.py
@@ -13,17 +13,33 @@
 NX, NZ, NY = 4, 8, 4
 PLANE = NX * NY * 2
 PROBES = 8
-CHUNKS = 2
+CHUNKS = 4
 N = BS // CHUNKS
 HALF = N // 2
 W = N + HALF
 KP = 32
 SUBC = 256
 PLAN = (
-    (((0, 512, 0, 512), None),),
-    (((0, 512, 512, 512), 0), ((512, 512, 0, 1024), 1)),
+    (),
+    (("mul", 0, 512, 0, 512, 0, 32, 4),),
+    (),
+    (
+        ("mul", 0, 512, 512, 512, 0, 32, 4),
+        ("give", 0),
+        ("mul", 512, 256, 0, 1024, 0, 32, 4),
+        ("give", 1),
+        ("add", 0),
+        ("mul", 768, 256, 0, 1024, 0, 24, 4),
+        ("add", 1),
+        ("end", 0),
+        ("mul", 768, 256, 0, 1024, 24, 32, 4),
+        ("give", 2),
+        ("end", 1),
+        ("add", 2),
+        ("end", 2),
+    ),
 )
-RETURNS = ((0, 512), (512, 512))
+RETURNS = ((0, 512), (512, 256), (768, 256))
 MESH = pl.DeviceIdType.MESH
 F32 = jnp.float32
 BF16 = jnp.bfloat16
@@ -115,8 +131,14 @@
         return 0
 
     lax.fori_loop(1, PLANE, greet, 0)
-    for step in (1, NZ - 1):
-        pl.semaphore_signal(barrier, inc=1, device_id=(column(lax.rem(z + step, NZ)), y), device_id_type=MESH)
+    for kk, steps in ((0, (-2,)), (1, (-1, 1)), (2, (-2, 2)), (3, (-1, 1))):
+        @pl.when(k == kk)
+        def _():
+            for step in steps:
+                pl.semaphore_signal(
+                    barrier, inc=1, device_id=(column(lax.rem(z + step + NZ, NZ)), y), device_id_type=MESH
+                )
+
     for zz in range(NZ):
         @pl.when(jnp.logical_or(jnp.logical_not(is_source), z != zz))
         def _():
@@ -134,23 +156,22 @@
                 p = prob[:, at:at + N].astype(F32)
                 down[q][b, :, N:W] = jnp.concatenate([p[:, :HALF], p[:, HALF:]], axis=0).astype(BF16)
 
-    @pl.when(is_source)
-    def _():
-        pl.semaphore_wait(barrier, PLANE - 1 + 2 + NZ - 1)
-
-    @pl.when(jnp.logical_not(is_source))
-    def _():
-        pl.semaphore_wait(barrier, PLANE - 1 + 2 + NZ)
-
-    def send_up(q, src):
+    for kk, targets in ((0, 4 + NZ - 1), (1, NZ), (2, 3 + NZ), (3, NZ)):
+        @pl.when(k == kk)
+        def _():
+            pl.semaphore_wait(barrier, PLANE - 1 + targets)
+
+    def along(q, src, step, upward):
+        into, send, recv = (up, up_send, up_recv) if upward else (down, down_send, down_recv)
         return pltpu.make_async_remote_copy(
-            src_ref=src, dst_ref=up[q], send_sem=up_send.at[q], recv_sem=up_recv.at[q],
-            device_id=(column(lax.rem(z + 1, NZ)), y), device_id_type=MESH)
-
-    def send_down(q):
-        return pltpu.make_async_remote_copy(
-            src_ref=down[q], dst_ref=down[q], send_sem=down_send.at[q], recv_sem=down_recv.at[q],
-            device_id=(column(lax.rem(z + NZ - 1, NZ)), y), device_id_type=MESH)
+            src_ref=src, dst_ref=into[q], send_sem=send.at[q], recv_sem=recv.at[q],
+            device_id=(column(lax.rem(z + step + NZ, NZ)), y), device_id_type=MESH)
+
+    def from_source(q, step):
+        return along(q, down[q], step, step > 0)
+
+    def relays(q):
+        return [along(q, up[q], 2, True), along(q, up[q], 1, True), along(q, down[q], -1, False)]
 
     def to_peer(q, d):
         b, s, _p = plane_peer(d)
@@ -158,35 +179,46 @@
             src_ref=sbuf[q].at[pl.ds(2 * d, 2)], dst_ref=rbuf[q].at[pl.ds(2 * me, 2)],
             send_sem=a_send.at[q], recv_sem=a_recv.at[q], device_id=(b, s), device_id_type=MESH)
 
-    @pl.when(is_source)
-    def _():
-        for q in range(CHUNKS):
-            send_up(q, down[q]).start()
-            send_down(q).start()
-
-    for q in range(CHUNKS):
-        send_up(q, up[q]).wait_recv()
-
-        @pl.when(jnp.logical_not(is_source))
-        def _():
-            send_up(q, up[q]).start()
-            send_down(q).wait_recv()
-
-        @pl.when(k >= 2)
-        def _():
-            send_down(q).start()
-
+    def pick(q):
         rbuf[q][2 * me] = up[q][tab[SEL + 2 * me]]
         rbuf[q][2 * me + 1] = down[q][tab[SEL + 2 * me + 1]]
 
-        def pick(d, _):
+        def one(i, _):
+            d = lax.rem(i * 11, PLANE)
             _b, _s, p = plane_peer(d)
             sbuf[q][2 * d] = up[q][tab[SEL + 2 * p]]
             sbuf[q][2 * d + 1] = down[q][tab[SEL + 2 * p + 1]]
             to_peer(q, d).start()
             return 0
 
-        lax.fori_loop(1, PLANE, pick, 0)
+        lax.fori_loop(1, PLANE, one, 0)
+
+    @pl.when(is_source)
+    def _():
+        for q in range(CHUNKS):
+            for steps in ((2, -2), (1, -1)):
+                for step in steps:
+                    from_source(q, step).start()
+                for step in steps:
+                    from_source(q, step).wait_send()
+
+    for q in range(CHUNKS):
+        along(q, up[q], 1, True).wait_recv()
+
+        @pl.when(k == 2)
+        def _():
+            for copy in relays(q)[:2]:
+                copy.start()
+
+        @pl.when(jnp.logical_not(is_source))
+        def _():
+            along(q, down[q], -1, False).wait_recv()
+
+        @pl.when(k == 2)
+        def _():
+            relays(q)[2].start()
+
+        pick(q)
 
     res[TILES] = jnp.zeros((PROBES, BS), F32)
 
@@ -197,43 +229,49 @@
     def prepare(q):
         at = q * N
         line = lax.broadcasted_iota(jnp.int32, (8, N), 0)
-
-        def one(t, _):
-            def parts(g):
-                g = g.astype(F32)
-                sq = jnp.sum(g * g, axis=0, keepdims=True)
-                hi = sq.astype(BF16).astype(F32)
-                mid = (sq - hi).astype(BF16).astype(F32)
-                low = (sq - hi) - mid
-                split = jnp.where(line == 0, hi, jnp.where(line == 1, mid, jnp.where(line == 2, low, 0.0)))
-                ones = jnp.where(line < 3, 1.0, 0.0)
-                return g, split, ones
-
-            g, split, ones = parts(rbuf[q][tab[ROW_SLOT + t], :, 0:N])
-            rowm[t, :, at:at + N] = jnp.concatenate([-2.0 * g, split, ones], axis=0).astype(BF16)
-            both = rbuf[q][tab[COL_SLOT + t]]
-            g, split, ones = parts(both[:, 0:N])
-            colm[t, at:at + N, :] = jnp.swapaxes(jnp.concatenate([g, ones, split], axis=0), 0, 1).astype(BF16)
-            p = both[:, N:W].astype(F32)
-            pr[t, :, at:at + N] = jnp.concatenate([p[0:8], p[8:16]], axis=1).astype(BF16)
+        ones = jnp.where(line < 3, 1.0, 0.0)
+
+        def parts(g):
+            g = g.astype(F32)
+            sq = jnp.sum(g * g, axis=0, keepdims=True)
+            hi = sq.astype(BF16).astype(F32)
+            mid = (sq - hi).astype(BF16).astype(F32)
+            low = (sq - hi) - mid
+            return g, jnp.where(line == 0, hi, jnp.where(line == 1, mid, jnp.where(line == 2, low, 0.0)))
+
+        def some(u, _):
+            for v in range(4):
+                t = u * 4 + v
+                g, split = parts(rbuf[q][tab[ROW_SLOT + t], :, 0:N])
+                rowm[t, :, at:at + N] = jnp.concatenate([-2.0 * g, split, ones], axis=0).astype(BF16)
+                both = rbuf[q][tab[COL_SLOT + t]]
+                g, split = parts(both[:, 0:N])
+                colm[t, at:at + N, :] = jnp.swapaxes(jnp.concatenate([g, ones, split], axis=0), 0, 1).astype(BF16)
+                p = both[:, N:W].astype(F32)
+                pr[t, :, at:at + N] = jnp.concatenate([p[0:8], p[8:16]], axis=1).astype(BF16)
             return 0
 
-        lax.fori_loop(0, TILES, one, 0)
-
-    def compute(r0, rn, c0, cn):
-        def one(t, _):
+        lax.fori_loop(0, TILES // 4, some, 0)
+
+    def compute(r0, rn, c0, cn, t0, t1, per):
+        def one(t):
             row = rowm[t, :, r0:r0 + rn]
             tiles = [
                 wendland11(jnp.dot(colm[t, j:j + SUBC, :], row, preferred_element_type=F32))
                 for j in range(c0, c0 + cn, SUBC)
             ]
-            part = jnp.dot(pr[t, :, c0:c0 + cn], jnp.concatenate(tiles, axis=0), preferred_element_type=F32)
+            block = jnp.concatenate(tiles, axis=0) if len(tiles) > 1 else tiles[0]
+            part = jnp.dot(pr[t, :, c0:c0 + cn], block, preferred_element_type=F32)
             if c0 > 0:
                 part = part + res[t, :, r0:r0 + rn]
             res[t, :, r0:r0 + rn] = part
+
+        def some(u, _):
+            for v in range(per):
+                one(t0 + u * per + v)
             return 0
 
-        lax.fori_loop(0, TILES, one, 0)
+        lax.fori_loop(0, (t1 - t0) // per, some, 0)
 
     def give_back(a):
         r0, rn = RETURNS[a]
@@ -282,8 +320,9 @@
             zero = jnp.zeros((PROBES, step), F32)
             sums = lax.fori_loop(0, PLANE, one, (zero,) * (2 * B_DEV))
             for h in range(2):
-                for b in range(B_DEV):
-                    s2[a][h, b // 2, b % 2, :, w:w + step] = sums[h * B_DEV + b]
+                for pair in range(NY):
+                    at = h * B_DEV + 2 * pair
+                    s2[a][h, pair, :, w:w + step] = jnp.concatenate(sums[at:at + 2], axis=0).astype(BF16)
         for h, zz in ((0, z_up), (1, z_down)):
             for s in range(NY):
                 if h == 1:
@@ -311,31 +350,24 @@
         def _():
             pltpu.make_async_copy(r2[a], r2[a], c_recv.at[a]).wait()
 
+        total = r2[a][0].astype(F32)
+        for zz in range(1, NZ):
+            total = total + r2[a][zz].astype(F32)
         for b in range(2):
-            total = r2[a][0, b]
-            for zz in range(1, NZ):
-                total = total + r2[a][zz, b]
-            out[:, b * BS + r0:b * BS + r0 + rn] = total
+            out[:, b * BS + r0:b * BS + r0 + rn] = total[8 * b:8 * b + 8]
 
     for q in range(CHUNKS):
         land = all_but_one(rbuf[q])
         pltpu.make_async_copy(land, land, a_recv.at[q]).wait()
         prepare(q)
-        for rect, back in PLAN[q]:
-            compute(*rect)
-            if back is not None:
-                give_back(back)
-    for a in range(len(RETURNS)):
-        add_up(a)
-    for a in range(len(RETURNS)):
-        finish(a)
+        for what, *args in PLAN[q]:
+            {"mul": compute, "give": give_back, "add": add_up, "end": finish}[what](*args)
 
     for q in range(CHUNKS):
-        send_up(q, up[q]).wait_send()
-
-        @pl.when(k != 1)
-        def _():
-            send_down(q).wait_send()
+        @pl.when(k == 2)
+        def _():
+            for copy in relays(q):
+                copy.wait_send()
 
         left = all_but_one(sbuf[q])
         pltpu.make_async_copy(left, left, a_send.at[q]).wait()
@@ -358,8 +390,8 @@
         [pltpu.VMEM((B_DEV, 16, W), BF16)] * (2 * CHUNKS)
         + [pltpu.VMEM((2 * PLANE, 16, W), BF16)] * (2 * CHUNKS)
         + [pltpu.VMEM((PLANE, 16, rn), BF16) for _, rn in RETURNS] * 2
-        + [pltpu.VMEM((2, NY, 2, PROBES, rn), F32) for _, rn in RETURNS]
-        + [pltpu.VMEM((NZ, 2, PROBES, rn), F32) for _, rn in RETURNS]
+        + [pltpu.VMEM((2, NY, 16, rn), BF16) for _, rn in RETURNS]
+        + [pltpu.VMEM((NZ, 16, rn), BF16) for _, rn in RETURNS]
         + [
             pltpu.VMEM((TILES, KP, BS), BF16),
             pltpu.VMEM((TILES, BS, KP), BF16),

time: 184 us -> 153 us (0.83)
  Pallas kernels: 178 us -> 145 us
    pallas_call x1, Pallas kernels: 178 us -> 145 us  [per_device(): pl.pallas_call(kernel, out_shape=jax.ShapeDtypeStruct((PROBES, 2 * BS), F...]
where the time goes in v2:
time: 153 us; the launch traced here: 152 us
  Pallas kernels  145 us (95%)
  local copies, waits for them, and re-layouts  4.86 us (3%)
    pallas_call x1, Pallas kernels, per_device(): pl.pallas_call(kernel, out_shape=jax.ShapeDtypeStruct((PROBES, 2 * BS), F...  145 us
    unnamed x7, local copies, waits for them, and re-layouts  3.52 us

profile of v2, /device:TPU:28, one launch (start us, length us, event | category | flops | bytes accessed | tf_op | source)
XLA Modules:
  0.0 151.8 jit_solution(15771102462532847800)
XLA Ops:
  0.0 0.0 copy-start
  0.0 0.8 copy-done
  0.8 0.0 copy-start.1
  0.8 0.1 reshape.189
  0.9 0.6 copy-done.1
  1.5 0.1 reshape.190
  1.7 0.1 add_select_fusion.3
  1.9 0.1 pad_add_fusion.2
  1.9 0.2 select_reduce_fusion.1
  2.1 0.1 copy.14
  2.2 0.1 reshape.191
  2.4 0.2 select_reduce_fusion
  2.5 0.1 copy.15
  2.6 0.1 sub.66
  2.8 0.1 fusion.11
  2.9 0.1 select_reduce_fusion.2
  3.0 0.6 pad_add_fusion.1.tab
  3.6 0.0 copy-start.2
  3.6 0.7 copy-done.2
  4.3 0.7 copy.16.inv
  4.9 145.4 %shard_map.55 = f32[8,2048]{1,0:T(8,128)} custom-call(bf16[16,8192]{1,0:T(8,128)(2,1)} %feat.1, bf16[8,8192]{1,0:T(8,128)(2,1)} %prob.1, f32[16,1]{1,0:T(8,128)} %copy.16.inv, s32[256]{0:T(256)} %pad_add_fusion.1.tab), custom_call_target="tpu_custom_call" | custom-call | tf_op jit(solution)/shard_map/pallas_call | solution.py:404
  150.3 1.5 copy.18
  (5 shorter events, 0.1 us)
Async XLA Ops:
  0.0 0.8 copy-start
  0.8 0.8 copy-start.1
  3.6 0.7 copy-start.2

commit v3 on v2

--- a/solution.py
+++ b/solution.py
@@ -18,10 +18,11 @@
 HALF = N // 2
 W = N + HALF
 KP = 32
-SUBC = 256
+SUBC = 512
+EARLY = 2
 PLAN = (
-    (),
-    (("mul", 0, 512, 0, 512, 0, 32, 4),),
+    (("swap", 2),),
+    (("mul", 0, 512, 0, 512, 0, 8, 4), ("swap", 3), ("mul", 0, 512, 0, 512, 8, 32, 4)),
     (),
     (
         ("mul", 0, 512, 512, 512, 0, 32, 4),
@@ -43,7 +44,7 @@
 MESH = pl.DeviceIdType.MESH
 F32 = jnp.float32
 BF16 = jnp.bfloat16
-SEL, RSEL, ROW_SLOT, COL_SLOT, TILE_OF = 0, 64, 128, 160, 192
+SLOT_ROW, TILE_ROW, TABLE_ROWS = 8, 16, 16 + 2 * PLANE
 
 
 def wendland11(sq_dist):
@@ -66,37 +67,46 @@
     return k, z_up, z_down
 
 
-def tables(tile_rows, tile_cols):
-    x, z, y, c = place(lax.axis_index("blk"), lax.axis_index("sub"))
+def fill_table(tile_rows, tile_cols, table, x, z, y, c):
     _, z_up, z_down = sources_of(z, y)
-
-    def in_plane(tiles):
-        tiles = tiles.reshape(NX, NZ, 2, NY, TILES)
-        tiles = lax.dynamic_index_in_dim(tiles, z, 1, keepdims=False)
-        return tiles.transpose(0, 2, 1, 3).reshape(PLANE, TILES)
+    lane = lax.broadcasted_iota(jnp.int32, (8, 128), 1)
+    line = lax.broadcasted_iota(jnp.int32, (8, 128), 0)
+
+    def in_plane(ref):
+        return jnp.concatenate(
+            [ref[pl.ds((px * NZ + z) * 2 + pc, 1), :] for px in range(NX) for pc in range(2)], axis=0
+        )
 
     rows, cols = in_plane(tile_rows), in_plane(tile_cols)
-    ends = jnp.concatenate([rows, cols], axis=1)
-    owned = jnp.stack([(x * NZ + z_up) * 2 + c, (x * NZ + z_down) * 2 + c])
-    sel = jnp.sum(
-        jnp.where((ends // B_DEV)[:, None, :] == owned[None, :, None], (ends % B_DEV)[:, None, :], 0), axis=2
-    )
-    rsel = jnp.sum(
-        jnp.where((rows // B_DEV)[:, None, :] == owned[None, :, None], (rows % B_DEV + 1)[:, None, :], 0), axis=2
-    ) - 1
-    mine = lax.dynamic_index_in_dim(ends, (x * NY + y) * 2 + c, 0, keepdims=False)
-    owner = mine // B_DEV
-    ox, oz, oc = owner // (2 * NZ), (owner // 2) % NZ, owner % 2
-    oy = oz % NY
-    _, o_up, _ = sources_of(z, oy)
-    slot = ((ox * NY + oy) * 2 + oc) * 2 + jnp.where(oz == o_up, 0, 1)
-    row_slot = slot[:TILES]
-    hit = row_slot[None, :] == jnp.arange(2 * PLANE, dtype=jnp.int32)[:, None]
-    tile_of = jnp.min(jnp.where(hit, jnp.arange(TILES, dtype=jnp.int32)[None, :], TILES), axis=1)
-    return jnp.concatenate([sel.reshape(-1), rsel.reshape(-1), slot, tile_of]).astype(jnp.int32)
-
-
-def kernel(feat, prob, inv, tab, out, *scratch):
+    first = jnp.zeros((8, 128), jnp.int32)
+    for h, zz in ((0, z_up), (1, z_down)):
+        own = (x * NZ + zz) * 2 + c
+        is_row, is_col = (rows >> 3) == own, (cols >> 3) == own
+        want = jnp.where(is_row, rows & 7, 0) + jnp.where(is_col, cols & 7, 0)
+        back = jnp.where(is_row, (rows & 7) + 1, 0)
+        for yy in range(NY):
+            for base, what in ((0, want), (8, back)):
+                total = jnp.sum(jnp.where((lane >> 5) == yy, what, 0), axis=1, keepdims=True)
+                first = jnp.where(lane == base + h * NY + yy, total, first)
+    table[0:8, :] = first
+
+    def slots(ref):
+        owner = ref[pl.ds((x * NZ + z) * 2 + c, 1), :] >> 3
+        ox, oz, oc = owner >> 4, (owner >> 1) & 7, owner & 1
+        oy = oz & 3
+        k = (z - oy + NZ) & 3
+        o_up = (z - jnp.where(k > 0, k, 4) + NZ) & 7
+        return ((ox * NY + oy) * 2 + oc) * 2 + jnp.where(oz == o_up, 0, 1)
+
+    row_slot, col_slot = slots(tile_rows), slots(tile_cols)
+    table[SLOT_ROW:SLOT_ROW + 8, :] = jnp.where(line == 0, row_slot, jnp.where(line == 1, col_slot, 0))
+    for at in range(0, 2 * PLANE, 8):
+        hit = jnp.logical_and(row_slot == line + at, (lane >> 5) == y)
+        tile = jnp.min(jnp.where(hit, lane & 31, TILES), axis=1, keepdims=True)
+        table[TILE_ROW + at:TILE_ROW + at + 8, :] = jnp.broadcast_to(tile, (8, 128))
+
+
+def kernel(feat, prob, inv, tile_rows, tile_cols, out, *scratch):
     it = iter(scratch)
     down = [next(it) for _ in range(CHUNKS)]
     up = [next(it) for _ in range(CHUNKS)]
@@ -109,6 +119,7 @@
     rowm, colm, pr, res = next(it), next(it), next(it), next(it)
     up_send, up_recv, down_send, down_recv, a_send, a_recv = [next(it) for _ in range(6)]
     b_send, b_recv, c_send, c_recv = [next(it) for _ in range(4)]
+    table, tab, tab_sem = next(it), next(it), next(it)
 
     blk, sub = lax.axis_index("blk"), lax.axis_index("sub")
     x, z, y, c = place(blk, sub)
@@ -123,6 +134,12 @@
     def column(zz):
         return (x * NZ + zz) * 2 + c
 
+    def wanted(p, h):
+        return tab[(p // 8) * 2 + p % 2, h * NY + (p // 2) % 4]
+
+    def wanted_row(p, h):
+        return tab[(p // 8) * 2 + p % 2, 8 + h * NY + (p // 2) % 4]
+
     barrier = pltpu.get_barrier_semaphore()
 
     def greet(d, _):
@@ -148,7 +165,10 @@
 
     @pl.when(is_source)
     def _():
-        scale = inv[...]
+        line = lax.broadcasted_iota(jnp.int32, (16, N), 0)
+        scale = jnp.zeros((16, N), F32)
+        for f in range(16):
+            scale = jnp.where(line == f, inv[f], scale)
         for q in range(CHUNKS):
             for b in range(B_DEV):
                 at = b * BS + q * N
@@ -156,6 +176,9 @@
                 p = prob[:, at:at + N].astype(F32)
                 down[q][b, :, N:W] = jnp.concatenate([p[:, :HALF], p[:, HALF:]], axis=0).astype(BF16)
 
+    fill_table(tile_rows, tile_cols, table, x, z, y, c)
+    pltpu.make_async_copy(table, tab, tab_sem).start()
+
     for kk, targets in ((0, 4 + NZ - 1), (1, NZ), (2, 3 + NZ), (3, NZ)):
         @pl.when(k == kk)
         def _():
@@ -180,14 +203,14 @@
             send_sem=a_send.at[q], recv_sem=a_recv.at[q], device_id=(b, s), device_id_type=MESH)
 
     def pick(q):
-        rbuf[q][2 * me] = up[q][tab[SEL + 2 * me]]
-        rbuf[q][2 * me + 1] = down[q][tab[SEL + 2 * me + 1]]
+        rbuf[q][2 * me] = up[q][wanted(me, 0)]
+        rbuf[q][2 * me + 1] = down[q][wanted(me, 1)]
 
         def one(i, _):
             d = lax.rem(i * 11, PLANE)
             _b, _s, p = plane_peer(d)
-            sbuf[q][2 * d] = up[q][tab[SEL + 2 * p]]
-            sbuf[q][2 * d + 1] = down[q][tab[SEL + 2 * p + 1]]
+            sbuf[q][2 * d] = up[q][wanted(p, 0)]
+            sbuf[q][2 * d + 1] = down[q][wanted(p, 1)]
             to_peer(q, d).start()
             return 0
 
@@ -202,23 +225,31 @@
                 for step in steps:
                     from_source(q, step).wait_send()
 
-    for q in range(CHUNKS):
-        along(q, up[q], 1, True).wait_recv()
-
+    pltpu.make_async_copy(table, tab, tab_sem).wait()
+    def relayed(q):
         @pl.when(k == 2)
         def _():
+            along(q, up[q], 1, True).wait_recv()
             for copy in relays(q)[:2]:
                 copy.start()
-
-        @pl.when(jnp.logical_not(is_source))
-        def _():
             along(q, down[q], -1, False).wait_recv()
-
-        @pl.when(k == 2)
-        def _():
             relays(q)[2].start()
 
+    def exchange(q):
+        @pl.when(k != 2)
+        def _():
+            along(q, up[q], 1, True).wait_recv()
+
+        @pl.when(jnp.logical_or(k == 1, k == 3))
+        def _():
+            along(q, down[q], -1, False).wait_recv()
+
         pick(q)
+
+    for q in range(CHUNKS):
+        relayed(q)
+        if q < EARLY:
+            exchange(q)
 
     res[TILES] = jnp.zeros((PROBES, BS), F32)
 
@@ -242,9 +273,9 @@
         def some(u, _):
             for v in range(4):
                 t = u * 4 + v
-                g, split = parts(rbuf[q][tab[ROW_SLOT + t], :, 0:N])
+                g, split = parts(rbuf[q][tab[SLOT_ROW, y * TILES + t], :, 0:N])
                 rowm[t, :, at:at + N] = jnp.concatenate([-2.0 * g, split, ones], axis=0).astype(BF16)
-                both = rbuf[q][tab[COL_SLOT + t]]
+                both = rbuf[q][tab[SLOT_ROW + 1, y * TILES + t]]
                 g, split = parts(both[:, 0:N])
                 colm[t, at:at + N, :] = jnp.swapaxes(jnp.concatenate([g, ones, split], axis=0), 0, 1).astype(BF16)
                 p = both[:, N:W].astype(F32)
@@ -283,7 +314,7 @@
                 device_id=(b, s), device_id_type=MESH)
 
         def packed(p):
-            both = [res[tab[TILE_OF + 2 * p + h], :, r0:r0 + rn] * 11.0 for h in range(2)]
+            both = [res[tab[TILE_ROW + 2 * p + h, 0], :, r0:r0 + rn] for h in range(2)]
             return jnp.concatenate(both, axis=0).astype(BF16)
 
         r1[a][me] = packed(me)
@@ -311,10 +342,10 @@
                 got = r1[a][p, :, w:w + step].astype(F32)
                 new = []
                 for h in range(2):
-                    which = tab[RSEL + 2 * p + h]
+                    which = wanted_row(p, h)
                     term = got[8 * h:8 * h + 8]
                     for b in range(B_DEV):
-                        new.append(sums[h * B_DEV + b] + jnp.where(which == b, term, 0.0))
+                        new.append(sums[h * B_DEV + b] + jnp.where(which == b + 1, term, 0.0))
                 return tuple(new)
 
             zero = jnp.zeros((PROBES, step), F32)
@@ -353,6 +384,7 @@
         total = r2[a][0].astype(F32)
         for zz in range(1, NZ):
             total = total + r2[a][zz].astype(F32)
+        total = total * 11.0
         for b in range(2):
             out[:, b * BS + r0:b * BS + r0 + rn] = total[8 * b:8 * b + 8]
 
@@ -361,7 +393,7 @@
         pltpu.make_async_copy(land, land, a_recv.at[q]).wait()
         prepare(q)
         for what, *args in PLAN[q]:
-            {"mul": compute, "give": give_back, "add": add_up, "end": finish}[what](*args)
+            {"mul": compute, "give": give_back, "add": add_up, "end": finish, "swap": exchange}[what](*args)
 
     for q in range(CHUNKS):
         @pl.when(k == 2)
@@ -382,7 +414,6 @@
 
 
 def per_device(features, probes, inv_scale, tile_rows, tile_cols):
-    tab = tables(tile_rows, tile_cols)
     vmem, smem = pl.BlockSpec(memory_space=pltpu.VMEM), pl.BlockSpec(memory_space=pltpu.SMEM)
     nr = len(RETURNS)
     dma = pltpu.SemaphoreType.DMA
@@ -400,17 +431,18 @@
         ]
         + [dma((CHUNKS,))] * 6
         + [dma((nr,))] * 4
+        + [pltpu.VMEM((TABLE_ROWS, 128), jnp.int32), pltpu.SMEM((TABLE_ROWS, 128), jnp.int32), dma]
     )
     return pl.pallas_call(
         kernel,
         out_shape=jax.ShapeDtypeStruct((PROBES, 2 * BS), F32),
-        in_specs=[vmem, vmem, vmem, smem],
+        in_specs=[vmem, vmem, smem, vmem, vmem],
         out_specs=vmem,
         scratch_shapes=scratch,
         compiler_params=pltpu.CompilerParams(
             collective_id=0, has_side_effects=True, vmem_limit_bytes=56 * 1024 * 1024
         ),
-    )(features, probes, inv_scale.reshape(-1, 1), tab)
+    )(features, probes, inv_scale, tile_rows.reshape(-1, 128), tile_cols.reshape(-1, 128))
 
 
 def solution(mesh):

time: 153 us -> 148 us (0.967)
  local copies, waits for them, and re-layouts: 4.86 us -> 1.47 us
    unnamed x7 -> x1, local copies, waits for them, and re-layouts: 3.52 us -> 1.47 us
where the time goes in v3:
time: 148 us; the launch traced here: 146 us
  Pallas kernels  145 us (98%)
    pallas_call x1, Pallas kernels, per_device(): pl.pallas_call(kernel, out_shape=jax.ShapeDtypeStruct((PROBES, 2 * BS), F...  145 us

profile of v3, /device:TPU:28, one launch (start us, length us, event | category | flops | bytes accessed | tf_op | source)
XLA Modules:
  0.0 146.0 jit_solution(8047833008288045865)
XLA Ops:
  0.0 144.5 %shard_map.55 = f32[8,2048]{1,0:T(8,128)} custom-call(bf16[16,8192]{1,0:T(8,128)(2,1)} %feat.1, bf16[8,8192]{1,0:T(8,128)(2,1)} %prob.1, f32[16]{0:T(128)} %inv.1, s32[64,128]{1,0:T(8,128)} %bitcast.2, s32[64,128]{1,0:T(8,128)} %bitcast.3), custom_call_target="tpu_custom_call" | custom-call | tf_op jit(solution)/shard_map/pallas_call | solution.py:436
  144.5 1.5 %copy.7 = f32[8,2048]{1,0:T(8,128)} copy(f32[8,2048]{1,0:T(8,128)} %shard_map.55) | data formatting | bytes 131072

commit v4 on v3

--- a/solution.py
+++ b/solution.py
@@ -134,6 +134,24 @@
     def column(zz):
         return (x * NZ + zz) * 2 + c
 
+    ys = [lax.rem(y + dy, NY) for dy in range(NY)]
+    cs = [c, 1 - c]
+
+    def each_peer(body):
+        def some(u, _):
+            for dy in range(NY):
+                for dc in range(2):
+                    dx = lax.rem(u + dy + 2 * dc, NX)
+                    px = lax.rem(x + dx, NX)
+                    at = (dx * 8 + dy * 2 + dc, px, ys[dy], cs[dc])
+                    if dy + dc:
+                        body(*at)
+                    else:
+                        pl.when(u != 0)(functools.partial(body, *at))
+            return 0
+
+        lax.fori_loop(0, NX, some, 0)
+
     def wanted(p, h):
         return tab[(p // 8) * 2 + p % 2, h * NY + (p // 2) % 4]
 
@@ -196,8 +214,7 @@
     def relays(q):
         return [along(q, up[q], 2, True), along(q, up[q], 1, True), along(q, down[q], -1, False)]
 
-    def to_peer(q, d):
-        b, s, _p = plane_peer(d)
+    def to_peer(q, d, b, s):
         return pltpu.make_async_remote_copy(
             src_ref=sbuf[q].at[pl.ds(2 * d, 2)], dst_ref=rbuf[q].at[pl.ds(2 * me, 2)],
             send_sem=a_send.at[q], recv_sem=a_recv.at[q], device_id=(b, s), device_id_type=MESH)
@@ -206,15 +223,12 @@
         rbuf[q][2 * me] = up[q][wanted(me, 0)]
         rbuf[q][2 * me + 1] = down[q][wanted(me, 1)]
 
-        def one(i, _):
-            d = lax.rem(i * 11, PLANE)
-            _b, _s, p = plane_peer(d)
-            sbuf[q][2 * d] = up[q][wanted(p, 0)]
-            sbuf[q][2 * d + 1] = down[q][wanted(p, 1)]
-            to_peer(q, d).start()
-            return 0
-
-        lax.fori_loop(1, PLANE, one, 0)
+        def one(d, px, py, pc):
+            sbuf[q][2 * d] = up[q][tab[px * 2 + pc, py]]
+            sbuf[q][2 * d + 1] = down[q][tab[px * 2 + pc, NY + py]]
+            to_peer(q, d, (px * NZ + z) * 2 + pc, py).start()
+
+        each_peer(one)
 
     @pl.when(is_source)
     def _():
@@ -307,25 +321,19 @@
     def give_back(a):
         r0, rn = RETURNS[a]
 
-        def copy(d):
-            b, s, _p = plane_peer(d)
-            return pltpu.make_async_remote_copy(
+        def packed(slot):
+            both = [res[tab[TILE_ROW + slot + h, 0], :, r0:r0 + rn] for h in range(2)]
+            return jnp.concatenate(both, axis=0).astype(BF16)
+
+        r1[a][me] = packed(2 * me)
+
+        def one(d, px, py, pc):
+            s1[a][d] = packed(px * 16 + py * 4 + pc * 2)
+            pltpu.make_async_remote_copy(
                 src_ref=s1[a].at[d], dst_ref=r1[a].at[me], send_sem=b_send.at[a], recv_sem=b_recv.at[a],
-                device_id=(b, s), device_id_type=MESH)
-
-        def packed(p):
-            both = [res[tab[TILE_ROW + 2 * p + h, 0], :, r0:r0 + rn] for h in range(2)]
-            return jnp.concatenate(both, axis=0).astype(BF16)
-
-        r1[a][me] = packed(me)
-
-        def one(d, _):
-            _b, _s, p = plane_peer(d)
-            s1[a][d] = packed(p)
-            copy(d).start()
-            return 0
-
-        lax.fori_loop(1, PLANE, one, 0)
+                device_id=((px * NZ + z) * 2 + pc, py), device_id_type=MESH).start()
+
+        each_peer(one)
 
     def second(a, h, s, zz):
         return pltpu.make_async_remote_copy(

time: 148 us -> 145 us (0.980)
  Pallas kernels: 145 us -> 142 us
    pallas_call x1, Pallas kernels: 145 us -> 142 us  [per_device(): pl.pallas_call(kernel, out_shape=jax.ShapeDtypeStruct((PROBES, 2 * BS), F...]
where the time goes in v4:
time: 145 us; the launch traced here: 144 us
  Pallas kernels  142 us (98%)
  local copies, waits for them, and re-layouts  1.47 us (1%)
    pallas_call x1, Pallas kernels, per_device(): pl.pallas_call(kernel, out_shape=jax.ShapeDtypeStruct((PROBES, 2 * BS), F...  142 us

profile of v4, /device:TPU:28, one launch (start us, length us, event | category | flops | bytes accessed | tf_op | source)
XLA Modules:
  0.0 143.6 jit_solution(702775886850693309)
XLA Ops:
  0.0 142.1 %shard_map.55 = f32[8,2048]{1,0:T(8,128)} custom-call(bf16[16,8192]{1,0:T(8,128)(2,1)} %feat.1, bf16[8,8192]{1,0:T(8,128)(2,1)} %prob.1, f32[16]{0:T(128)} %inv.1, s32[64,128]{1,0:T(8,128)} %bitcast.2, s32[64,128]{1,0:T(8,128)} %bitcast.3), custom_call_target="tpu_custom_call" | custom-call | tf_op jit(solution)/shard_map/pallas_call | solution.py:444
  142.1 1.5 %copy.7 = f32[8,2048]{1,0:T(8,128)} copy(f32[8,2048]{1,0:T(8,128)} %shard_map.55) | data formatting | bytes 131072
